TPU v7x, 768 devices: a whole 4x8x12 slice. The times are simulated.
768 devices in a mesh: dom: 12 (over z), grp: 64 (over x, y, core).
Axes of the slice: x: 4, y: 8, z: 12, core: 2. Of those that a mesh axis runs over, the one named last changes fastest.
Arguments:
- a_blocks: bfloat16 [18432, 7, 4096], P(('dom', 'grp')), may hold values from -0.75 to 0.75
- p_blocks: bfloat16 [18432, 4096], P(('dom', 'grp')), may hold values from -1.1953125 to 1.1953125
- columns: int32 [18432, 7], P(('dom', 'grp')), may hold values from 0 to 18431, as said below
- targets: int32 [18432, 7], P(('dom', 'grp')), may hold values from 0 to 24575, as said below
Outputs:
- coarse: float32 [24576, 4096], P(('dom', 'grp'))
Inputs may be any that keep to these rules, and one draw needn't show every extreme that they name: `columns`: slot 0 of element e is e itself. Every other entry of an element held by device index r (elements r * 24 to (r + 1) * 24 - 1, devices in dom-major order) names an element of device r, one of the last 6 elements of device r - 64, or one of the first 6 elements of device r + 64, the latter two only where that device exists. `targets`: A target of an element of device r names a coarse block of device r or of another device with the same dom index (blocks q * 32 to (q + 1) * 32 - 1 belong to device q). Of the entries of one device, at most 2 name blocks of any one other device; for each dom index some device receives exactly 2 from every other device of that dom index.
All inputs are finite; a program needn't handle non-finite values.
Results may differ from a plain program's by a relative error of at most 0.0029.
Values may be sent and summed in bfloat16 or wider, within the bound.
A program may use at most 64 MiB of HBM per device.

v0:
```python
import jax
import jax.numpy as jnp
from jax import lax
from jax.sharding import PartitionSpec as P

BS = 64
CAP = 2
CB_DEV = 32


def with_halo(array, sides, width):
    for axis, dim in sides:
        size, length = (lax.axis_size(axis), array.shape[dim])
        up = [(i, (i + 1) % size) for i in range(size - 1)]
        down = [(j, i) for i, j in up]
        last = lax.slice_in_dim(array, length - width, length, axis=dim)
        leading = lax.slice_in_dim(array, 0, width, axis=dim)
        before = lax.ppermute(last, axis, up)
        after = lax.ppermute(leading, axis, down)
        array = jnp.concatenate([before, array, after], axis=dim)
    return array


def on_device(a_blocks, p_blocks, columns, targets):
    n_grp = lax.axis_size("grp")
    elems, count, area = a_blocks.shape
    units = elems * count
    rim = elems // 4
    me = lax.axis_index("dom") * n_grp + lax.axis_index("grp")
    padded = with_halo(p_blocks, (("dom", 0),), rim)
    owner = columns // elems
    offset = columns - owner * elems
    apart = owner - me
    index = jnp.where(
        apart == 0, offset + rim, jnp.where(apart < 0, offset - (elems - rim), offset + rim + elems)
    )
    neighbours = padded[index.reshape(units)].reshape(units, BS, BS)
    matrices = a_blocks.reshape(units, BS, BS)
    product = jnp.einsum(
        "uij,ujk->uik", matrices, neighbours, preferred_element_type=jnp.float32
    ).astype(jnp.bfloat16)
    pieces = p_blocks.reshape(elems, BS, BS)
    terms = jnp.einsum(
        "eji,ekjl->ekil",
        pieces,
        product.reshape(elems, count, BS, BS),
        preferred_element_type=jnp.float32,
    ).reshape(units, area)
    flat_target = targets.reshape(units)
    block_device = flat_target // CB_DEV
    at_home = block_device == me
    peer = block_device % n_grp
    column = flat_target - block_device * CB_DEV
    chosen = (
        (peer[:, None] == jnp.arange(n_grp, dtype=jnp.int32)[None, :]) & (~at_home)[:, None]
    ).astype(jnp.int32)
    rank = jnp.sum((jnp.cumsum(chosen, axis=0) - chosen) * chosen, axis=1)
    place = jnp.where(at_home, n_grp * CAP, peer * CAP + rank)
    labels_out = (
        jnp.full((n_grp * CAP,), -1, jnp.int32)
        .at[place]
        .set(column, mode="drop")
        .reshape(n_grp, CAP)
    )
    home_slot = jnp.where(at_home, column, CB_DEV)
    coarse = jax.ops.segment_sum(terms, home_slot, num_segments=CB_DEV + 1)[:CB_DEV]
    own_rep = jnp.repeat(p_blocks, count, axis=0)
    stacked = jnp.stack([product.reshape(units, area), own_rep], axis=1)
    payload = jnp.zeros((n_grp * CAP, 2, area), jnp.bfloat16).at[place].set(stacked, mode="drop")
    sent = lax.all_to_all(
        payload.reshape(n_grp, CAP, 2, area), "grp", split_axis=0, concat_axis=0, tiled=True
    )
    labels = lax.all_to_all(labels_out, "grp", split_axis=0, concat_axis=0, tiled=True)
    groups = sent.shape[0]
    items = sent.shape[1]
    right = sent[:, :, 0].reshape(groups, items, BS, BS)
    left = sent[:, :, 1].reshape(groups, items, BS, BS)
    made = jnp.einsum("gcji,gcjl->gcil", left, right, preferred_element_type=jnp.float32)
    received, labels = (made.reshape(groups, items, area), labels)
    flat_labels = labels.reshape(-1)
    incoming_slot = jnp.where(flat_labels < 0, CB_DEV, flat_labels)
    coarse = (
        coarse
        + jax.ops.segment_sum(received.reshape(-1, area), incoming_slot, num_segments=CB_DEV + 1)[
            :CB_DEV
        ]
    )
    return coarse


def solution(mesh):
    in_specs = (
        P(("dom", "grp"), None, None),
        P(("dom", "grp"), None),
        P(("dom", "grp"), None),
        P(("dom", "grp"), None),
    )
    out_specs = P(("dom", "grp"), None)
    return jax.shard_map(
        on_device, mesh=mesh, in_specs=in_specs, out_specs=out_specs, check_vma=False
    )
```

profile of v0, /device:TPU:193, one launch (start us, length us, event | category | flops | bytes accessed | tf_op | source)
XLA Modules:
  0.0 181.6 jit_solution(1191749806083958221)
XLA Ops:
  0.0 0.8 copy.21
  2.1 1.1 scatter_custom_fusion.1
  4.0 10.8 %all-to-all-start = ((s32[64,1,2]{2,1,0:T(1,128)}), s32[64,1,2]{2,1,0:T(1,128)S(1)}, u32[]{:S(2)}, u32[]{:S(2)}) async-start(s32[64,1,2]{2,1,0:T(1,128)} %bitcast.10), calls=%async_computation | async-start | bytes 65536 | tf_op jit(solution)/shard_map/all_to_all | solution.py:73
  14.8 0.9 fusion.18
  15.7 5.2 %collective-permute-start = (bf16[6,4096]{1,0:T(8,128)(2,1)S(1)}, bf16[6,4096]{1,0:T(8,128)(2,1)S(1)}, u32[]{:S(2)}, u32[]{:S(2)}) collective-permute-start(bf16[6,4096]{1,0:T(8,128)(2,1)S(1)} %get-tuple-element.11), channel_id=1, source_target_pairs={{0,64},{64,128},{128,192},{192,256},{256,320},{320,384},{384,448},... | collective-permute-start | bytes 147464 | tf_op jit(solution)/shard_map/ppermute | solution.py:18
  20.9 1.9 %collective-permute-start.1 = (bf16[6,4096]{1,0:T(8,128)(2,1)S(1)}, bf16[6,4096]{1,0:T(8,128)(2,1)S(1)}, u32[]{:S(2)}, u32[]{:S(2)}) collective-permute-start(bf16[6,4096]{1,0:T(8,128)(2,1)S(1)} %get-tuple-element.12), channel_id=1, source_target_pairs={{64,0},{128,64},{192,128},{256,192},{320,256},{384,320},{448,384},... | collective-permute-start | bytes 147464 | tf_op jit(solution)/shard_map/ppermute | solution.py:19
  23.7 2.1 %copy.24 = bf16[24,7,4096]{2,1,0:T(8,128)(2,1)S(1)} copy(bf16[24,7,4096]{2,0,1:T(8,128)(2,1)} %param.4) | data formatting | bytes 2752512 | tf_op args[0]
  25.8 4.2 %reshape.270 = bf16[168,64,64]{2,1,0:T(8,128)(2,1)} reshape(bf16[24,7,4096]{2,1,0:T(8,128)(2,1)S(1)} %copy.24) | data formatting | bytes 2752512 | tf_op jit(solution)/shard_map/reshape | solution.py:38
  30.7 2.5 %copy.32 = bf16[168,1,4096]{0,2,1:T(8,128)(2,1)} copy(bf16[168,1,4096]{2,0,1:T(8,128)(2,1)S(1)} %stack_reshape.7) | data formatting | bytes 2752512 | tf_op jit(solution)/shard_map/stack;reshape | solution.py:68
  33.3 1.4 gather_fusion
  34.7 1.9 %copy.23 = bf16[168,4096]{0,1:T(8,128)(2,1)S(1)} copy(bf16[168,4096]{1,0:T(8,128)(2,1)S(1)} %gather_fusion) | data formatting | bytes 2752512 | tf_op jit(solution)/shard_map/gather | solution.py:37
  36.6 4.8 %copy.25 = bf16[168,64,64]{1,2,0:T(8,128)(2,1)} copy(bf16[168,64,64]{0,2,1:T(8,128)(2,1)S(1)} %bitcast.48) | data formatting | bytes 2752512 | tf_op jit(solution)/shard_map/reshape | solution.py:37
  41.4 4.2 %convolution_convert_fusion = bf16[168,64,64]{2,1,0:T(8,128)(2,1)S(1)} fusion(bf16[168,64,64]{1,2,0:T(8,128)(2,1)} %copy.25, bf16[168,64,64]{2,1,0:T(8,128)(2,1)} %reshape.270), kind=kOutput, calls=%fused_computation.7 | convolution fusion | flops 88768512 | bytes 4128768 | tf_op jit(solution)/shard_map/uij,ujk->uik/dot_general | solution.py:39
  45.6 5.3 %copy.31 = bf16[168,64,64]{0,2,1:T(8,128)(2,1)} copy(bf16[168,64,64]{1,2,0:T(8,128)(2,1)S(1)} %bitcast.45) | data formatting | bytes 2752512 | tf_op jit(solution)/shard_map/convert_element_type | solution.py:41
  50.9 5.0 %pad_maximum_fusion = bf16[168,2,4096]{0,2,1:T(8,128)(2,1)} fusion(bf16[168,1,4096]{0,2,1:T(8,128)(2,1)} %copy.32, bf16[168,1,4096]{0,2,1:T(8,128)(2,1)} %bitcast.49), kind=kLoop, calls=%fused_computation.5 | loop fusion | flops 1376256 | bytes 5505024 | tf_op jit(solution)/shard_map/stack | solution.py:68
  55.9 8.5 %copy.33 = bf16[168,2,4096]{2,1,0:T(2,128)(2,1)} copy(bf16[168,2,4096]{0,2,1:T(8,128)(2,1)} %pad_maximum_fusion) | data formatting | bytes 5505024 | tf_op jit(solution)/shard_map/stack | solution.py:68
  64.4 3.4 %broadcast_in_dim.30 = bf16[128,2,4096]{2,1,0:T(2,128)(2,1)} broadcast(bf16[]{:T(256)} %constant.77.clone.1), dimensions={} | broadcast | bytes 2097154 | tf_op jit(solution)/shard_map/broadcast_in_dim | solution.py:69
  67.8 24.1 %scatter_fusion = bf16[128,2,4096]{2,1,0:T(2,128)(2,1)} fusion(bf16[128,2,4096]{2,1,0:T(2,128)(2,1)} %broadcast_in_dim.30, s32[168]{0:T(256)S(1)} %bitcast.51, bf16[168,2,4096]{2,1,0:T(2,128)(2,1)} %copy.33), kind=kCustom, calls=%fused_computation.3 | custom fusion | bytes 8258208 | tf_op jit(solution)/shard_map/scatter | solution.py:69
  92.0 5.1 %copy.34 = bf16[64,2,2,4096]{3,1,2,0:T(2,128)(2,1)} copy(bf16[64,2,2,4096]{3,2,1,0:T(2,128)(2,1)} %bitcast.47) | data formatting | bytes 4194304 | tf_op jit(solution)/shard_map/reshape | solution.py:71
  97.0 11.2 %all-to-all-start.1 = ((bf16[64,2,2,4096]{3,1,2,0:T(2,128)(2,1)}), bf16[64,2,2,4096]{3,1,2,0:T(2,128)(2,1)}, u32[]{:S(2)}, u32[]{:S(2)}) async-start(bf16[64,2,2,4096]{3,1,2,0:T(2,128)(2,1)} %copy.34), calls=%async_computation.1 | async-start | bytes 4194304 | tf_op jit(solution)/shard_map/all_to_all | solution.py:70
  110.0 3.2 %convolution_bitcast_fusion = f32[24,7,64,64]{2,3,1,0:T(8,128)} fusion(bf16[24,7,64,64]{2,3,1,0:T(8,128)(2,1)S(1)} %bitcast.46, bf16[24,64,64,1]{2,1,0,3:T(8,128)(2,1)S(1)} %reshape.320), kind=kOutput, calls=%fused_computation.6 | convolution fusion | flops 88080384 | bytes 4325376 | tf_op jit(solution)/shard_map/eji,ekjl->ekil/dot_general | solution.py:43
  113.2 6.1 %copy.26 = f32[24,7,64,64]{3,2,1,0:T(8,128)} copy(f32[24,7,64,64]{2,3,1,0:T(8,128)} %convolution_bitcast_fusion) | data formatting | bytes 5505024 | tf_op jit(solution)/shard_map/eji,ekjl->ekil/transpose | solution.py:43
  119.4 4.2 %reshape.292 = f32[168,4096]{1,0:T(8,128)S(1)} reshape(f32[24,7,64,64]{3,2,1,0:T(8,128)} %copy.26) | data formatting | bytes 5505024 | tf_op jit(solution)/shard_map/reshape | solution.py:48
  123.5 4.9 %scatter_custom_fusion = f32[33,4096]{1,0:T(8,128)} fusion(s32[168]{0:T(256)S(1)} %bitcast.54, f32[168,4096]{1,0:T(8,128)S(1)} %reshape.292, f32[]{:T(128)} %constant.35.clone.1), kind=kCustom, calls=%fused_computation.13 | custom fusion | flops 688128 | bytes 540676 | tf_op jit(solution)/shard_map/scatter-add | solution.py:66
  128.4 30.9 %all-to-all-done.1 = bf16[64,2,2,4096]{3,1,2,0:T(2,128)(2,1)} async-done(((bf16[64,2,2,4096]{3,1,2,0:T(2,128)(2,1)}), bf16[64,2,2,4096]{3,1,2,0:T(2,128)(2,1)}, u32[]{:S(2)}, u32[]{:S(2)}) %all-to-all-start.1) | async-done | bytes 2097184 | tf_op jit(solution)/shard_map/all_to_all | solution.py:70
  159.3 3.9 %fusion.17 = (bf16[64,2,1,4096]{3,1,2,0:T(2,128)(2,1)}, bf16[64,2,1,4096]{3,1,2,0:T(2,128)(2,1)S(1)}) fusion(bf16[64,2,2,4096]{3,1,2,0:T(2,128)(2,1)} %all-to-all-done.1), kind=kLoop, calls=%fused_computation.61 | loop fusion | bytes 4194304 | tf_op jit(solution)/shard_map/slice | solution.py:76
  163.2 3.8 %reshape_squeeze.7 = bf16[64,2,64,64]{3,2,1,0:T(8,128)(2,1)S(1)} reshape(bf16[64,2,1,4096]{3,1,2,0:T(2,128)(2,1)} %get-tuple-element.9) | data formatting | bytes 2097152 | tf_op jit(solution)/shard_map/reshape;squeeze | solution.py:76
  167.0 2.4 %reshape.322 = bf16[64,2,64,64]{3,2,1,0:T(8,128)(2,1)} reshape(bf16[64,2,1,4096]{3,1,2,0:T(2,128)(2,1)S(1)} %get-tuple-element.10) | data formatting | bytes 2097152 | tf_op jit(solution)/shard_map/reshape;squeeze | solution.py:77
  169.4 4.4 %fusion.19 = f32[64,2,64,64]{3,2,1,0:T(8,128)} fusion(bf16[64,2,64,64]{3,2,1,0:T(8,128)(2,1)} %reshape.322, bf16[64,2,64,64]{3,2,1,0:T(8,128)(2,1)S(1)} %reshape_squeeze.7), kind=kOutput, calls=%fused_computation.63 | convolution fusion | flops 67108864 | bytes 4194304 | tf_op jit(solution)/shard_map/gcji,gcjl->gcil/dot_general | solution.py:78
  173.8 3.6 %reshape.316 = f32[128,4096]{1,0:T(8,128)S(1)} reshape(f32[64,2,64,64]{3,2,1,0:T(8,128)} %fusion.19) | data formatting | bytes 4194304 | tf_op jit(solution)/shard_map/reshape;reshape | solution.py:84
  177.4 3.4 %scatter_custom_fusion.3 = f32[33,4096]{1,0:T(8,128)S(1)} fusion(s32[128]{0:T(128)S(1)} %fusion.14, f32[128,4096]{1,0:T(8,128)S(1)} %reshape.316, f32[]{:T(128)} %constant.35.clone.1), kind=kCustom, calls=%fused_computation.11 | custom fusion | flops 524288 | bytes 540676 | tf_op jit(solution)/shard_map/scatter-add | solution.py:84
  180.8 0.8 slice_add_fusion
  (38 shorter events, 5.4 us)
Async XLA Ops:
  4.0 93.0 %all-to-all-start = ((s32[64,1,2]{2,1,0:T(1,128)}), s32[64,1,2]{2,1,0:T(1,128)S(1)}, u32[]{:S(2)}, u32[]{:S(2)}) async-start(s32[64,1,2]{2,1,0:T(1,128)} %bitcast.10), calls=%async_computation | async-start | bytes 65536 | tf_op jit(solution)/shard_map/all_to_all | solution.py:73
  15.7 17.5 %collective-permute-start = (bf16[6,4096]{1,0:T(8,128)(2,1)S(1)}, bf16[6,4096]{1,0:T(8,128)(2,1)S(1)}, u32[]{:S(2)}, u32[]{:S(2)}) collective-permute-start(bf16[6,4096]{1,0:T(8,128)(2,1)S(1)} %get-tuple-element.11), channel_id=1, source_target_pairs={{0,64},{64,128},{128,192},{192,256},{256,320},{320,384},{384,448},... | collective-permute-start | bytes 147464 | tf_op jit(solution)/shard_map/ppermute | solution.py:18
  20.9 12.3 %collective-permute-start.1 = (bf16[6,4096]{1,0:T(8,128)(2,1)S(1)}, bf16[6,4096]{1,0:T(8,128)(2,1)S(1)}, u32[]{:S(2)}, u32[]{:S(2)}) collective-permute-start(bf16[6,4096]{1,0:T(8,128)(2,1)S(1)} %get-tuple-element.12), channel_id=1, source_target_pairs={{64,0},{128,64},{192,128},{256,192},{320,256},{384,320},{448,384},... | collective-permute-start | bytes 147464 | tf_op jit(solution)/shard_map/ppermute | solution.py:19
  25.8 4.2 %copy-start = (bf16[24,4096]{1,0:T(8,128)(2,1)S(1)}, bf16[24,4096]{1,0:T(8,128)(2,1)}, u32[]{:S(2)}) copy-start(bf16[24,4096]{1,0:T(8,128)(2,1)} %param.5) | copy-start | bytes 589828
  97.0 11.2 %copy-start.1 = (bf16[24,4096]{1,0:T(8,128)(2,1)S(1)}, bf16[24,4096]{1,0:T(8,128)(2,1)}, u32[]{:S(2)}) copy-start(bf16[24,4096]{1,0:T(8,128)(2,1)} %param.5) | copy-start | bytes 589828
  97.0 62.3 %all-to-all-start.1 = ((bf16[64,2,2,4096]{3,1,2,0:T(2,128)(2,1)}), bf16[64,2,2,4096]{3,1,2,0:T(2,128)(2,1)}, u32[]{:S(2)}, u32[]{:S(2)}) async-start(bf16[64,2,2,4096]{3,1,2,0:T(2,128)(2,1)} %copy.34), calls=%async_computation.1 | async-start | bytes 4194304 | tf_op jit(solution)/shard_map/all_to_all | solution.py:70
  173.8 7.0 %copy-start.2 = (f32[33,4096]{1,0:T(8,128)S(1)}, f32[33,4096]{1,0:T(8,128)}, u32[]{:S(2)}) copy-start(f32[33,4096]{1,0:T(8,128)} %scatter_custom_fusion) | copy-start | bytes 1622020
where the time goes:
time: 183 us; the launch traced here: 182 us
  local copies, waits for them, and re-layouts  93.1 us (51%)
  waiting for transfers between devices  30.9 us (17%)
  starting transfers between devices  29.1 us (16%)
  other arithmetic  16.5 us (9%)
  matrix products  11.8 us (6%)
    all_to_all x1, waiting for transfers between devices, on_device(): lax.all_to_all(payload.reshape(n_grp, CAP, 2, area), 'grp', split_axis=0,...  30.9 us
    scatter x1, local copies, waits for them, and re-layouts, on_device(): jnp.zeros((n_grp * CAP, 2, area), jnp.bfloat16).at[place]  24.1 us
    another operation x3, local copies, waits for them, and re-layouts, on_device(): stacked = jnp.stack([product.reshape(units, area), own_rep], axis=1)  11.4 us
    all_to_all x1, starting transfers between devices, on_device(): lax.all_to_all(payload.reshape(n_grp, CAP, 2, area), 'grp', split_axis=0,...  11.2 us
    all_to_all x1, starting transfers between devices, on_device(): lax.all_to_all(labels_out, 'grp', split_axis=0, concat_axis=0, tiled=True)  10.8 us
    transpose x1, local copies, waits for them, and re-layouts, on_device(): jnp.einsum('eji,ekjl->ekil', pieces, product.reshape(elems, count, BS, BS...  6.15 us
    convert_element_type x1, local copies, waits for them, and re-layouts, on_device(): product = jnp.einsum('uij,ujk->uik', matrices, neighbours, preferred_elem...  5.34 us
    ppermute x1, starting transfers between devices, with_halo(): before = lax.ppermute(last, axis, up)  5.21 us
  transfers between devices with their start and end apart: 4, of which 1 were waited for; matrix products, arithmetic and copies ran while one was open for 52% of the time, Pallas kernels for 0%

commit v1 on v0

v1 whole, which is shorter than its diff:
```python
import functools

import jax
import jax.numpy as jnp
from jax import lax
from jax.experimental import pallas as pl
from jax.experimental.pallas import tpu as pltpu
from jax.sharding import PartitionSpec as P

MESH = pl.DeviceIdType.MESH
F32 = jnp.float32
BF16 = jnp.bfloat16
I32 = jnp.int32

E = 24
K = 7
HALO = 6
CB = 32
CAP = 2
NG = 64
R = 32
L = 128
UNITS = E * K
NP = E + 2 * HALO


def iota(shape, dim):
    return lax.broadcasted_iota(I32, shape, dim)


def split(u):
    k = (u * 2731) >> 16
    return k, u - k * E


def peer_of(me, d):
    return lax.rem(me + d, NG)


def routing(tgt_v, device):
    t = tgt_v[...]
    owner = t >> 5
    col = t & (CB - 1)
    home = owner == device
    dest = jnp.where(home, NG, owner & (NG - 1)).astype(F32)
    key = jnp.where(home, col, CB).astype(F32)
    colf = col.astype(F32)
    unit_k, unit_e = split(iota((UNITS, K), 0)), split(iota((UNITS, E), 0))
    spread = jnp.where(unit_k[0] == iota((UNITS, K), 1), 1.0, 0.0).astype(F32)
    mine = unit_e[1] == iota((UNITS, E), 1)

    def column(x):
        wide = jnp.dot(spread, x, preferred_element_type=F32)
        return jnp.sum(jnp.where(mine, wide, 0.0), axis=1, keepdims=True)

    dest_c = column(dest)
    key_c = column(key)
    col_c = column(colf)
    pick = jnp.where(split(iota((E, UNITS), 1))[1] == iota((E, UNITS), 0), 1.0, 0.0).astype(F32)
    wide = jnp.dot(key, pick, preferred_element_type=F32)
    mine_r = split(iota((K, UNITS), 1))[0] == iota((K, UNITS), 0)
    key_r = jnp.sum(jnp.where(mine_r, wide, 0.0), axis=0, keepdims=True)
    unit_c = iota((UNITS, 1), 0).astype(F32)
    chosen = dest_c == iota((UNITS, L), 1).astype(F32)
    chosen = jnp.where(iota((UNITS, L), 1) < NG, jnp.where(chosen, 1.0, 0.0), 0.0)
    before = jnp.where(iota((UNITS, UNITS), 1) < iota((UNITS, UNITS), 0), 1.0, 0.0)
    rank = jnp.dot(before.astype(BF16), chosen.astype(BF16), preferred_element_type=F32)
    first = jnp.where(rank == 0.0, chosen, 0.0)
    second = jnp.where(rank == 1.0, chosen, 0.0)

    def row(x):
        return jnp.sum(x, axis=0, keepdims=True)

    rows = [
        row(first * unit_c),
        row(second * unit_c),
        row(first * (col_c - CB)) + CB,
        row(second * (col_c - CB)) + CB,
    ]
    full_c = key_c * 256.0 + unit_c
    full_r = key_r * 256.0 + iota((1, UNITS), 1).astype(F32)
    rank_c = jnp.sum(jnp.where(full_r < full_c, 1.0, 0.0), axis=1, keepdims=True)
    at = jnp.where(rank_c == iota((UNITS, 2 * L), 1).astype(F32), 1.0, 0.0)
    perm = row(at * unit_c)
    skey = row(at * key_c)
    slot = iota((UNITS, L), 1).astype(F32)
    upto = row(jnp.where(key_c <= slot, 1.0, 0.0))
    count = row(jnp.where(key_c == slot, 1.0, 0.0))
    rows += [perm[:, :L], perm[:, L:], skey[:, :L], skey[:, L:], jnp.maximum(upto - 1.0, 0.0), jnp.minimum(count, 1.0)]
    rows += [jnp.zeros((1, L), F32)] * (16 - len(rows))
    return jnp.concatenate(rows, axis=0).astype(I32)


def exchange(a_ref, p_ref, col_ref, tgt_ref, recv_ref, lab_ref, home_ref,
             a_v, p_v, col_s, tgt_v, tab_v, tab_s, pf, p2, std_a, std_b, w, ptx, af, a2,
             send_v, lab_v, acc_v, home_v,
             a_sem, p_sem, small_sem, halo_send, halo_recv, pay_send, pay_recv, lab_send, lab_recv):
    dom, me = lax.axis_index("dom"), lax.axis_index("grp")
    doms = lax.axis_size("dom")
    device = dom * NG + me
    has_low = dom > 0
    has_high = dom < doms - 1

    barrier = pltpu.get_barrier_semaphore()

    @pl.when(has_low)
    def _():
        pl.semaphore_signal(barrier, inc=1, device_id=(dom - 1, me), device_id_type=MESH)

    @pl.when(has_high)
    def _():
        pl.semaphore_signal(barrier, inc=1, device_id=(dom + 1, me), device_id_type=MESH)

    def greet(d, c):
        pl.semaphore_signal(barrier, inc=1, device_id=(dom, peer_of(me, d)), device_id_type=MESH)
        return c

    lax.fori_loop(1, NG, greet, 0)

    p_copy = pltpu.make_async_copy(p_ref, p_v, p_sem)
    p_copy.start()
    tgt_copy = pltpu.make_async_copy(tgt_ref, tgt_v, small_sem.at[0])
    tgt_copy.start()
    col_copy = pltpu.make_async_copy(col_ref, col_s, small_sem.at[1])
    col_copy.start()
    a_copies = [
        pltpu.make_async_copy(a_ref.at[i], a_v.at[i], a_sem.at[i]) for i in range(K)
    ]
    for c in a_copies:
        c.start()

    p_copy.wait()
    for r in range(R):
        pf[pl.ds(r * E, E), :] = p_v[:, r * L:(r + 1) * L].astype(F32)

    def own(e, c):
        p2[HALO + e] = pf[pl.ds(e, R, stride=E), :].astype(BF16)
        return c

    lax.fori_loop(0, E, own, 0, unroll=4)

    @pl.when(jnp.logical_not(has_low))
    def _():
        p2[pl.ds(0, HALO)] = jnp.zeros((HALO, R, L), BF16)

    @pl.when(jnp.logical_not(has_high))
    def _():
        p2[pl.ds(HALO + E, HALO)] = jnp.zeros((HALO, R, L), BF16)

    left = iota((64, L), 1) < 64
    left32 = iota((R, L), 1) < 64

    def spread_block(c, x):
        xr = pltpu.roll(x, 64, 1)
        std_a[pl.ds(0, R, stride=2), :] = x
        std_a[pl.ds(1, R, stride=2), :] = xr
        std_b[pl.ds(0, R, stride=2), :] = xr
        std_b[pl.ds(1, R, stride=2), :] = x
        lo = jnp.where(left, std_a[0:64, :], 0.0).astype(BF16)
        hi = jnp.where(left, 0.0, std_b[0:64, :]).astype(BF16)
        w[c, 0:64, 0:L] = lo
        w[c, 0:64, L:2 * L] = hi
        w[c, 64:128, 0:L] = hi
        w[c, 64:128, L:2 * L] = lo

    pl.semaphore_wait(barrier, NG - 1 + has_low.astype(I32) + has_high.astype(I32))

    def halo(up):
        src = p2.at[pl.ds(E, HALO)] if up else p2.at[pl.ds(HALO, HALO)]
        dst = p2.at[pl.ds(0, HALO)] if up else p2.at[pl.ds(HALO + E, HALO)]
        i = 0 if up else 1
        return pltpu.make_async_remote_copy(
            src_ref=src, dst_ref=dst, send_sem=halo_send.at[i], recv_sem=halo_recv.at[i],
            device_id=(dom + 1 if up else dom - 1, me), device_id_type=MESH)

    @pl.when(has_high)
    def _():
        halo(True).start()

    @pl.when(has_low)
    def _():
        halo(False).start()

    tgt_copy.wait()
    tab_v[...] = routing(tgt_v, device)
    tab_copy = pltpu.make_async_copy(tab_v, tab_s, small_sem.at[2])
    tab_copy.start()

    to = iota((L, L), 1)
    moved = jnp.where(iota((L, L), 0) == (to & 64) + ((to & 31) << 1) + ((to >> 5) & 1), 1.0, 0.0).astype(BF16)

    def prepare(e, c):
        x = pf[pl.ds(e, R, stride=E), :]
        spread_block(HALO + e, x)
        x = jnp.dot(x.astype(BF16), moved, preferred_element_type=F32)
        stacked = jnp.concatenate(
            [x, pltpu.roll(x, 32, 1), pltpu.roll(x, 64, 1), pltpu.roll(x, 96, 1)], axis=0)
        ptx[e] = stacked.T[0:R, :].astype(BF16)
        return c

    lax.fori_loop(0, E, prepare, 0)

    def unpack(k, c):
        for r in range(R):
            af[pl.ds(r * E, E), :] = a_v[k, :, r * L:(r + 1) * L].astype(F32)
        for e in range(E):
            a2[k * E + e] = af[pl.ds(e, R, stride=E), :].astype(BF16)
        return c

    for i in range(K):
        a_copies[i].wait()
    lax.fori_loop(0, K, unpack, 0)
    col_copy.wait()
    tab_copy.wait()

    @pl.when(has_low)
    def _():
        halo(True).wait_recv()

    @pl.when(has_high)
    def _():
        halo(False).wait_recv()

    def prepare_halo(i, c):
        at = jnp.where(i < HALO, i, i + E)
        spread_block(at, p2[at].astype(F32))
        return c

    lax.fori_loop(0, 2 * HALO, prepare_halo, 0)

    first_own = device * E

    def term(u):
        u = jnp.clip(u, 0, UNITS - 1)
        k, e = split(u)
        rel = col_s[k, e] - first_own
        at = jnp.where(rel < 0, rel + NG * E - (E - HALO), jnp.where(rel < E, rel + HALO, rel - NG * E + HALO + E))
        at = jnp.clip(at, 0, NP - 1)
        out = jnp.dot(a2[u], w[at], preferred_element_type=F32)
        one, two = out[:, :L], out[:, L:]
        right = jnp.concatenate(
            [jnp.where(left32, one, 0.0), jnp.where(left32, 0.0, one),
             jnp.where(left32, two, 0.0), jnp.where(left32, 0.0, two)], axis=0).astype(BF16)
        return jnp.dot(ptx[e], right, preferred_element_type=F32)

    def pay(d):
        return pltpu.make_async_remote_copy(
            src_ref=send_v.at[d], dst_ref=recv_ref.at[d], send_sem=pay_send, recv_sem=pay_recv,
            device_id=(dom, peer_of(me, d)), device_id_type=MESH)

    def lab(d):
        return pltpu.make_async_remote_copy(
            src_ref=lab_v.at[d], dst_ref=lab_ref.at[d], send_sem=lab_send, recv_sem=lab_recv,
            device_id=(dom, peer_of(me, d)), device_id_type=MESH)

    lane = iota((1, L), 1)
    group = 3

    def send(i, c):
        for j in range(group):
            d = 1 + i * group + j
            q = peer_of(me, d)
            for s in range(CAP):
                send_v[d, s * R:(s + 1) * R, :] = term(tab_s[s, q]).astype(BF16)
            lab_v[d] = jnp.where(lane == 0, tab_s[2, q], tab_s[3, q])
        for j in range(group):
            d = 1 + i * group + j
            pay(d).start()
            lab(d).start()
        return c

    lax.fori_loop(0, (NG - 1) // group, send, 0)

    def at_home(i, acc):
        n = i * 4
        terms = []
        for j in range(4):
            pos = n + j
            terms.append(term(tab_s[4 + pos // L, lax.rem(pos, L)]))
        for j in range(4):
            pos = n + j
            prev = jnp.maximum(pos - 1, 0)
            same = (tab_s[6 + pos // L, lax.rem(pos, L)] == tab_s[6 + prev // L, lax.rem(prev, L)]).astype(F32)
            acc = acc * same + terms[j]
            acc_v[pos] = acc
        return acc

    lax.fori_loop(0, E * K // 4, at_home, jnp.zeros((R, L), F32))

    def fetch(t, c):
        home_v[t] = acc_v[jnp.clip(tab_s[8, t], 0, UNITS - 1)] * tab_s[9, t].astype(F32)
        return c

    lax.fori_loop(0, CB, fetch, 0, unroll=4)
    home_copy = pltpu.make_async_copy(home_v, home_ref, small_sem.at[3])
    home_copy.start()

    def all_pay():
        return pltpu.make_async_remote_copy(
            src_ref=send_v.at[pl.ds(1, NG - 1)], dst_ref=recv_ref.at[pl.ds(1, NG - 1)], send_sem=pay_send,
            recv_sem=pay_recv, device_id=(dom, peer_of(me, 1)), device_id_type=MESH)

    def all_lab():
        return pltpu.make_async_remote_copy(
            src_ref=lab_v.at[pl.ds(1, NG - 1)], dst_ref=lab_ref.at[pl.ds(1, NG - 1)], send_sem=lab_send,
            recv_sem=lab_recv, device_id=(dom, peer_of(me, 1)), device_id_type=MESH)

    @pl.when(has_high)
    def _():
        halo(True).wait_send()

    @pl.when(has_low)
    def _():
        halo(False).wait_send()

    home_copy.wait()
    all_lab().wait()
    all_pay().wait()


def collect(recv_ref, lab_ref, home_ref, out_ref, recv_v, lab_s, acc, turned, rsem, lsem, hsem):
    lab_copy = pltpu.make_async_copy(lab_ref, lab_s, lsem)
    lab_copy.start()
    home_copy = pltpu.make_async_copy(home_ref, acc.at[pl.ds(0, CB)], hsem)
    home_copy.start()
    copies = [pltpu.make_async_copy(recv_ref.at[pl.ds(i * 8, 8)], recv_v.at[pl.ds(i * 8, 8)], rsem.at[i]) for i in range(8)]
    for c in copies:
        c.start()
    lab_copy.wait()
    home_copy.wait()

    def add(d, c):
        for s in range(CAP):
            t = jnp.clip(lab_s[d, 0, s], 0, CB)
            acc[t] = acc[t] + recv_v[d, s * R:(s + 1) * R, :].astype(F32)
        return c

    for i in range(8):
        copies[i].wait()
        lax.fori_loop(max(1, i * 8), i * 8 + 8, add, 0)

    def turn(t, c):
        turned[pl.ds(t, R, stride=CB), :] = acc[t]
        return c

    lax.fori_loop(0, CB, turn, 0, unroll=4)
    for r in range(R):
        out_ref[:, r * L:(r + 1) * L] = turned[r * CB:(r + 1) * CB, :]


def on_device(a_blocks, p_blocks, columns, targets):
    hbm = pl.BlockSpec(memory_space=pl.ANY)
    dma = pltpu.SemaphoreType.DMA
    recv, labels, home = pl.pallas_call(
        exchange,
        out_shape=(
            jax.ShapeDtypeStruct((NG, CAP * R, L), BF16),
            jax.ShapeDtypeStruct((NG, 1, L), I32),
            jax.ShapeDtypeStruct((CB, R, L), F32),
        ),
        in_specs=[hbm] * 4,
        out_specs=(hbm, hbm, hbm),
        scratch_shapes=[
            pltpu.VMEM((K, E, 64 * 64), BF16),
            pltpu.VMEM((E, 64 * 64), BF16),
            pltpu.SMEM((K, E), I32),
            pltpu.VMEM((K, E), I32),
            pltpu.VMEM((16, L), I32),
            pltpu.SMEM((16, L), I32),
            pltpu.VMEM((R * E + E, L), F32),
            pltpu.VMEM((NP, R, L), BF16),
            pltpu.VMEM((72, L), F32),
            pltpu.VMEM((72, L), F32),
            pltpu.VMEM((NP, L, 2 * L), BF16),
            pltpu.VMEM((E, R, L), BF16),
            pltpu.VMEM((R * E + E, L), F32),
            pltpu.VMEM((UNITS, R, L), BF16),
            pltpu.VMEM((NG, CAP * R, L), BF16),
            pltpu.VMEM((NG, 1, L), I32),
            pltpu.VMEM((E * K, R, L), F32),
            pltpu.VMEM((CB, R, L), F32),
            dma((K,)), dma, dma((4,)), dma((2,)), dma((2,)), dma, dma, dma, dma,
        ],
        compiler_params=pltpu.CompilerParams(
            collective_id=0, has_side_effects=True, vmem_limit_bytes=62 * 1024 * 1024),
    )(a_blocks.transpose(1, 0, 2), p_blocks, columns.T, targets.T)
    return pl.pallas_call(
        collect,
        out_shape=jax.ShapeDtypeStruct((CB, 64 * 64), F32),
        in_specs=[hbm] * 3,
        out_specs=pl.BlockSpec(memory_space=pltpu.VMEM),
        scratch_shapes=[
            pltpu.VMEM((NG, CAP * R, L), BF16),
            pltpu.SMEM((NG, 1, L), I32),
            pltpu.VMEM((CB + 1, R, L), F32),
            pltpu.VMEM((R * CB + CB, L), F32),
            dma((8,)), dma, dma,
        ],
        compiler_params=pltpu.CompilerParams(vmem_limit_bytes=62 * 1024 * 1024),
    )(recv, labels, home)


def solution(mesh):
    spec = P(("dom", "grp"), None)
    return jax.shard_map(
        on_device, mesh=mesh, in_specs=(P(("dom", "grp"), None, None), spec, spec, spec), out_specs=spec,
        check_vma=False)
```

time: 183 us -> 54.1 us (0.30)
  the two profiles are of different devices: /device:TPU:193 before, /device:TPU:1 now
where the time goes in v1:
time: 54.1 us; the launch traced here: 53.9 us
  Pallas kernels  53.9 us (100%)
    pallas_call x1, Pallas kernels, on_device(): pl.pallas_call(exchange, out_shape=(jax.ShapeDtypeStruct((NG, CAP * R, L)...  50.2 us
    pallas_call x1, Pallas kernels, on_device(): pl.pallas_call(collect, out_shape=jax.ShapeDtypeStruct((CB, 64 * 64), F32...  3.69 us

profile of v1, /device:TPU:1, one launch (start us, length us, event | category | flops | bytes accessed | tf_op | source)
XLA Modules:
  0.0 53.9 jit_solution(8235730801328915965)
XLA Ops:
  0.0 50.2 %shard_map.46 = (bf16[64,64,128]{2,1,0:T(8,128)(2,1)}, s32[64,1,128]{2,1,0:T(1,128)}, f32[32,32,128]{2,1,0:T(8,128)}) custom-call(bf16[7,24,4096]{2,1,0:T(8,128)(2,1)} %bitcast.3, bf16[24,4096]{1,0:T(8,128)(2,1)} %p_ref.1, s32[7,24]{1,0:T(8,128)} %bitcast.4, s32[7,24]{1,0:T(8,128)} %bitcast.5), custom_call_target="tpu_custom_call" | custom-call | tf_op jit(solution)/shard_map/pallas_call | solution.py:354
  50.2 3.7 %shard_map.47 = f32[32,4096]{1,0:T(8,128)} custom-call(bf16[64,64,128]{2,1,0:T(8,128)(2,1)} %get-tuple-element.8.recv_ref, s32[64,1,128]{2,1,0:T(1,128)} %get-tuple-element.9.lab_ref, f32[32,32,128]{2,1,0:T(8,128)} %get-tuple-element.10.home_ref), custom_call_target="tpu_custom_call" | custom-call | tf_op jit(solution)/shard_map/pallas_call | solution.py:387

commit v2 on v1

--- a/solution.py
+++ b/solution.py
@@ -33,8 +33,8 @@
     return k, u - k * E
 
 
-def peer_of(me, d):
-    return lax.rem(me + d, NG)
+def kind_of(dom, g):
+    return jnp.where((dom == 0) & (g == 0), 2, jnp.where(((g >> 1) & 7) == 4, 1, 0))
 
 
 def routing(tgt_v, device):
@@ -92,40 +92,47 @@
 
 
 def exchange(a_ref, p_ref, col_ref, tgt_ref, recv_ref, lab_ref, home_ref,
-             a_v, p_v, col_s, tgt_v, tab_v, tab_s, pf, p2, std_a, std_b, w, ptx, af, a2,
+             a_v, p_v, col_s, tgt_v, tab_v, tab_s, pf, p2, w, ptx, af, a2,
              send_v, lab_v, acc_v, home_v,
-             a_sem, p_sem, small_sem, halo_send, halo_recv, pay_send, pay_recv, lab_send, lab_recv):
+             a_sem, p_sem, small_sem, halo_send, halo_recv, pay_send, pay_recv, lab_send, lab_recv, late, late_z):
     dom, me = lax.axis_index("dom"), lax.axis_index("grp")
     doms = lax.axis_size("dom")
     device = dom * NG + me
+    x, y, core = me >> 4, (me >> 1) & 7, me & 1
+    kind = kind_of(dom, me)
     has_low = dom > 0
     has_high = dom < doms - 1
-
-    barrier = pltpu.get_barrier_semaphore()
-
-    @pl.when(has_low)
-    def _():
-        pl.semaphore_signal(barrier, inc=1, device_id=(dom - 1, me), device_id_type=MESH)
-
-    @pl.when(has_high)
-    def _():
-        pl.semaphore_signal(barrier, inc=1, device_id=(dom + 1, me), device_id_type=MESH)
-
-    def greet(d, c):
-        pl.semaphore_signal(barrier, inc=1, device_id=(dom, peer_of(me, d)), device_id_type=MESH)
-        return c
-
-    lax.fori_loop(1, NG, greet, 0)
+    above_first = (dom == 1) & (me == 0)
 
     p_copy = pltpu.make_async_copy(p_ref, p_v, p_sem)
     p_copy.start()
+
+    barrier = pltpu.get_barrier_semaphore()
+
+    @pl.when(has_low)
+    def _():
+        pl.semaphore_signal(barrier, inc=1, device_id=(dom - 1, me), device_id_type=MESH)
+
+    @pl.when(has_high & (kind < 2))
+    def _():
+        pl.semaphore_signal(barrier, inc=1, device_id=(dom + 1, me), device_id_type=MESH)
+
+    def greet(d, c):
+        q = (me + d) & (NG - 1)
+
+        @pl.when(kind <= kind_of(dom, q))
+        def _():
+            pl.semaphore_signal(barrier, inc=1, device_id=(dom, q), device_id_type=MESH)
+
+        return c
+
+    lax.fori_loop(1, NG, greet, 0)
+
     tgt_copy = pltpu.make_async_copy(tgt_ref, tgt_v, small_sem.at[0])
     tgt_copy.start()
     col_copy = pltpu.make_async_copy(col_ref, col_s, small_sem.at[1])
     col_copy.start()
-    a_copies = [
-        pltpu.make_async_copy(a_ref.at[i], a_v.at[i], a_sem.at[i]) for i in range(K)
-    ]
+    a_copies = [pltpu.make_async_copy(a_ref.at[i], a_v.at[i], a_sem.at[i]) for i in range(K)]
     for c in a_copies:
         c.start()
 
@@ -137,7 +144,7 @@
         p2[HALO + e] = pf[pl.ds(e, R, stride=E), :].astype(BF16)
         return c
 
-    lax.fori_loop(0, E, own, 0, unroll=4)
+    lax.fori_loop(0, E, own, 0, unroll=8)
 
     @pl.when(jnp.logical_not(has_low))
     def _():
@@ -146,24 +153,6 @@
     @pl.when(jnp.logical_not(has_high))
     def _():
         p2[pl.ds(HALO + E, HALO)] = jnp.zeros((HALO, R, L), BF16)
-
-    left = iota((64, L), 1) < 64
-    left32 = iota((R, L), 1) < 64
-
-    def spread_block(c, x):
-        xr = pltpu.roll(x, 64, 1)
-        std_a[pl.ds(0, R, stride=2), :] = x
-        std_a[pl.ds(1, R, stride=2), :] = xr
-        std_b[pl.ds(0, R, stride=2), :] = xr
-        std_b[pl.ds(1, R, stride=2), :] = x
-        lo = jnp.where(left, std_a[0:64, :], 0.0).astype(BF16)
-        hi = jnp.where(left, 0.0, std_b[0:64, :]).astype(BF16)
-        w[c, 0:64, 0:L] = lo
-        w[c, 0:64, L:2 * L] = hi
-        w[c, 64:128, 0:L] = hi
-        w[c, 64:128, L:2 * L] = lo
-
-    pl.semaphore_wait(barrier, NG - 1 + has_low.astype(I32) + has_high.astype(I32))
 
     def halo(up):
         src = p2.at[pl.ds(E, HALO)] if up else p2.at[pl.ds(HALO, HALO)]
@@ -173,32 +162,76 @@
             src_ref=src, dst_ref=dst, send_sem=halo_send.at[i], recv_sem=halo_recv.at[i],
             device_id=(dom + 1 if up else dom - 1, me), device_id_type=MESH)
 
-    @pl.when(has_high)
-    def _():
-        halo(True).start()
-
-    @pl.when(has_low)
-    def _():
-        halo(False).start()
+    def met():
+        early = 7 * 8 - (dom == 0).astype(I32)
+        peers = jnp.where(kind == 0, early - 1, jnp.where(kind == 1, early + 8 - 1, NG - 1))
+        low = (has_low & jnp.logical_not(above_first)).astype(I32)
+        pl.semaphore_wait(barrier, peers + low + has_high.astype(I32))
+
+    def send_halo():
+        @pl.when(has_high)
+        def _():
+            halo(True).start()
+
+        @pl.when(above_first)
+        def _():
+            pl.semaphore_wait(late_z, 1)
+
+        @pl.when(has_low)
+        def _():
+            halo(False).start()
+
+    @pl.when(kind > 0)
+    def _():
+        met()
+
+        @pl.when(kind == 2)
+        def _():
+            pl.semaphore_signal(late_z, inc=1, device_id=(dom + 1, me), device_id_type=MESH)
+
+        send_halo()
+
+        def answer(d, c):
+            q = (me + d) & (NG - 1)
+
+            @pl.when(kind_of(dom, q) < kind)
+            def _():
+                pl.semaphore_signal(late.at[kind - 1], inc=1, device_id=(dom, q), device_id_type=MESH)
+
+            return c
+
+        lax.fori_loop(1, NG, answer, 0)
 
     tgt_copy.wait()
     tab_v[...] = routing(tgt_v, device)
     tab_copy = pltpu.make_async_copy(tab_v, tab_s, small_sem.at[2])
     tab_copy.start()
 
-    to = iota((L, L), 1)
-    moved = jnp.where(iota((L, L), 0) == (to & 64) + ((to & 31) << 1) + ((to >> 5) & 1), 1.0, 0.0).astype(BF16)
+    left = iota((R, L), 1) < 64
+    row64, col64 = iota((64, 64), 0), iota((64, 64), 1)
+    woven = jnp.where(row64 == ((col64 & 31) << 1) + (col64 >> 5), 1.0, 0.0).astype(BF16)
+    even = jnp.where(iota((R, L), 1) == iota((R, L), 0) * 2, 1.0, 0.0).astype(BF16)
+
+    def spread_block(c, b):
+        br = pltpu.roll(b, 64, 1)
+        parts = jnp.concatenate(
+            [jnp.concatenate([jnp.where(left, b, 0.0), jnp.where(left, 0.0, br)], axis=1),
+             jnp.concatenate([jnp.where(left, br, 0.0), jnp.where(left, 0.0, b)], axis=1)], axis=0).astype(BF16)
+        z = jnp.dot(woven, parts, preferred_element_type=F32).astype(BF16)
+        w[c, 0:64, :] = z
+        w[c, 64:128, 0:L] = z[:, L:]
+        w[c, 64:128, L:2 * L] = z[:, :L]
 
     def prepare(e, c):
-        x = pf[pl.ds(e, R, stride=E), :]
-        spread_block(HALO + e, x)
-        x = jnp.dot(x.astype(BF16), moved, preferred_element_type=F32)
+        b = pf[pl.ds(e, R, stride=E), :]
+        spread_block(HALO + e, b)
         stacked = jnp.concatenate(
-            [x, pltpu.roll(x, 32, 1), pltpu.roll(x, 64, 1), pltpu.roll(x, 96, 1)], axis=0)
-        ptx[e] = stacked.T[0:R, :].astype(BF16)
-        return c
-
-    lax.fori_loop(0, E, prepare, 0)
+            [b, pltpu.roll(b, 63, 1), pltpu.roll(b, 64, 1), pltpu.roll(b, 127, 1)], axis=0).astype(BF16)
+        ptx[e] = lax.dot_general(
+            even, stacked, (((1,), (1,)), ((), ())), preferred_element_type=F32).astype(BF16)
+        return c
+
+    lax.fori_loop(0, E, prepare, 0, unroll=4)
 
     def unpack(k, c):
         for r in range(R):
@@ -213,6 +246,11 @@
     col_copy.wait()
     tab_copy.wait()
 
+    @pl.when(kind == 0)
+    def _():
+        met()
+        send_halo()
+
     @pl.when(has_low)
     def _():
         halo(True).wait_recv()
@@ -226,7 +264,7 @@
         spread_block(at, p2[at].astype(F32))
         return c
 
-    lax.fori_loop(0, 2 * HALO, prepare_halo, 0)
+    lax.fori_loop(0, 2 * HALO, prepare_halo, 0, unroll=4)
 
     first_own = device * E
 
@@ -239,53 +277,74 @@
         out = jnp.dot(a2[u], w[at], preferred_element_type=F32)
         one, two = out[:, :L], out[:, L:]
         right = jnp.concatenate(
-            [jnp.where(left32, one, 0.0), jnp.where(left32, 0.0, one),
-             jnp.where(left32, two, 0.0), jnp.where(left32, 0.0, two)], axis=0).astype(BF16)
+            [jnp.where(left, one, 0.0), jnp.where(left, 0.0, one),
+             jnp.where(left, two, 0.0), jnp.where(left, 0.0, two)], axis=0).astype(BF16)
         return jnp.dot(ptx[e], right, preferred_element_type=F32)
 
-    def pay(d):
+    def pay(q):
         return pltpu.make_async_remote_copy(
-            src_ref=send_v.at[d], dst_ref=recv_ref.at[d], send_sem=pay_send, recv_sem=pay_recv,
-            device_id=(dom, peer_of(me, d)), device_id_type=MESH)
-
-    def lab(d):
+            src_ref=send_v.at[q], dst_ref=recv_ref.at[me], send_sem=pay_send, recv_sem=pay_recv,
+            device_id=(dom, q), device_id_type=MESH)
+
+    def lab(q):
         return pltpu.make_async_remote_copy(
-            src_ref=lab_v.at[d], dst_ref=lab_ref.at[d], send_sem=lab_send, recv_sem=lab_recv,
-            device_id=(dom, peer_of(me, d)), device_id_type=MESH)
+            src_ref=lab_v.at[q], dst_ref=lab_ref.at[me], send_sem=lab_send, recv_sem=lab_recv,
+            device_id=(dom, q), device_id_type=MESH)
 
     lane = iota((1, L), 1)
-    group = 3
-
-    def send(i, c):
-        for j in range(group):
-            d = 1 + i * group + j
-            q = peer_of(me, d)
-            for s in range(CAP):
-                send_v[d, s * R:(s + 1) * R, :] = term(tab_s[s, q]).astype(BF16)
-            lab_v[d] = jnp.where(lane == 0, tab_s[2, q], tab_s[3, q])
-        for j in range(group):
-            d = 1 + i * group + j
-            pay(d).start()
-            lab(d).start()
-        return c
-
-    lax.fori_loop(0, (NG - 1) // group, send, 0)
+
+    def fill(q):
+        for s in range(CAP):
+            send_v[q, s * R:(s + 1) * R, :] = term(tab_s[s, q]).astype(BF16)
+        lab_v[q] = jnp.where(lane == 0, tab_s[2, q], tab_s[3, q])
+
+    ring = (y + 3) & 7
+
+    def send(n, c):
+        half, i = n >> 3, n & 7
+        away = jnp.where((i & 1) == 1, (i + 1) >> 1, 7 - (i >> 1))
+        to_y = jnp.where(i == 7, 4, (5 + lax.rem(ring + away, 7)) & 7)
+        peers = []
+        for j in range(4):
+            to_x, to_core = (x + half * 2 + j // 2) & 3, (core + j) & 1
+            peers.append((to_x * 8 + to_y) * 2 + to_core)
+        for q in peers:
+            fill(q)
+
+        @pl.when((n == 7) & (kind == 0))
+        def _():
+            pl.semaphore_wait(late.at[0], 8)
+
+        for q in peers:
+            @pl.when((q != me) & ((dom > 0) | (q > 0)))
+            def _():
+                pay(q).start()
+                lab(q).start()
+        return c
+
+    lax.fori_loop(0, 16, send, 0)
+
+    @pl.when((dom == 0) & (me > 0))
+    def _():
+        pl.semaphore_wait(late.at[1], 1)
+        pay(0).start()
+        lab(0).start()
 
     def at_home(i, acc):
-        n = i * 4
+        n = i * 8
         terms = []
-        for j in range(4):
+        for j in range(8):
             pos = n + j
-            terms.append(term(tab_s[4 + pos // L, lax.rem(pos, L)]))
-        for j in range(4):
+            terms.append(term(tab_s[4 + (pos >> 7), pos & 127]))
+        for j in range(8):
             pos = n + j
             prev = jnp.maximum(pos - 1, 0)
-            same = (tab_s[6 + pos // L, lax.rem(pos, L)] == tab_s[6 + prev // L, lax.rem(prev, L)]).astype(F32)
+            same = (tab_s[6 + (pos >> 7), pos & 127] == tab_s[6 + (prev >> 7), prev & 127]).astype(F32)
             acc = acc * same + terms[j]
             acc_v[pos] = acc
         return acc
 
-    lax.fori_loop(0, E * K // 4, at_home, jnp.zeros((R, L), F32))
+    lax.fori_loop(0, UNITS // 8, at_home, jnp.zeros((R, L), F32))
 
     def fetch(t, c):
         home_v[t] = acc_v[jnp.clip(tab_s[8, t], 0, UNITS - 1)] * tab_s[9, t].astype(F32)
@@ -297,13 +356,13 @@
 
     def all_pay():
         return pltpu.make_async_remote_copy(
-            src_ref=send_v.at[pl.ds(1, NG - 1)], dst_ref=recv_ref.at[pl.ds(1, NG - 1)], send_sem=pay_send,
-            recv_sem=pay_recv, device_id=(dom, peer_of(me, 1)), device_id_type=MESH)
+            src_ref=send_v.at[pl.ds(0, NG - 1)], dst_ref=recv_ref.at[pl.ds(0, NG - 1)], send_sem=pay_send,
+            recv_sem=pay_recv, device_id=(dom, me ^ 1), device_id_type=MESH)
 
     def all_lab():
         return pltpu.make_async_remote_copy(
-            src_ref=lab_v.at[pl.ds(1, NG - 1)], dst_ref=lab_ref.at[pl.ds(1, NG - 1)], send_sem=lab_send,
-            recv_sem=lab_recv, device_id=(dom, peer_of(me, 1)), device_id_type=MESH)
+            src_ref=lab_v.at[pl.ds(0, NG - 1)], dst_ref=lab_ref.at[pl.ds(0, NG - 1)], send_sem=lab_send,
+            recv_sem=lab_recv, device_id=(dom, me ^ 1), device_id_type=MESH)
 
     @pl.when(has_high)
     def _():
@@ -318,32 +377,34 @@
     all_pay().wait()
 
 
-def collect(recv_ref, lab_ref, home_ref, out_ref, recv_v, lab_s, acc, turned, rsem, lsem, hsem):
+def collect(recv_ref, lab_ref, home_ref, out_ref, recv_v, lab_s, acc, acc_b, turned, rsem, lsem, hsem):
+    me = lax.axis_index("grp")
     lab_copy = pltpu.make_async_copy(lab_ref, lab_s, lsem)
     lab_copy.start()
     home_copy = pltpu.make_async_copy(home_ref, acc.at[pl.ds(0, CB)], hsem)
     home_copy.start()
-    copies = [pltpu.make_async_copy(recv_ref.at[pl.ds(i * 8, 8)], recv_v.at[pl.ds(i * 8, 8)], rsem.at[i]) for i in range(8)]
+    copies = [pltpu.make_async_copy(recv_ref.at[pl.ds(i * 16, 16)], recv_v.at[pl.ds(i * 16, 16)], rsem.at[i]) for i in range(4)]
     for c in copies:
         c.start()
+    acc_b[...] = jnp.zeros_like(acc_b)
     lab_copy.wait()
     home_copy.wait()
 
     def add(d, c):
-        for s in range(CAP):
-            t = jnp.clip(lab_s[d, 0, s], 0, CB)
-            acc[t] = acc[t] + recv_v[d, s * R:(s + 1) * R, :].astype(F32)
-        return c
-
-    for i in range(8):
+        for s, total in ((0, acc), (1, acc_b)):
+            t = jnp.where(d == me, CB, jnp.clip(lab_s[d, 0, s], 0, CB))
+            total[t] = total[t] + recv_v[d, s * R:(s + 1) * R, :].astype(F32)
+        return c
+
+    for i in range(4):
         copies[i].wait()
-        lax.fori_loop(max(1, i * 8), i * 8 + 8, add, 0)
+        lax.fori_loop(i * 16, i * 16 + 16, add, 0, unroll=8)
 
     def turn(t, c):
-        turned[pl.ds(t, R, stride=CB), :] = acc[t]
-        return c
-
-    lax.fori_loop(0, CB, turn, 0, unroll=4)
+        turned[pl.ds(t, R, stride=CB), :] = acc[t] + acc_b[t]
+        return c
+
+    lax.fori_loop(0, CB, turn, 0, unroll=8)
     for r in range(R):
         out_ref[:, r * L:(r + 1) * L] = turned[r * CB:(r + 1) * CB, :]
 
@@ -369,8 +430,6 @@
             pltpu.SMEM((16, L), I32),
             pltpu.VMEM((R * E + E, L), F32),
             pltpu.VMEM((NP, R, L), BF16),
-            pltpu.VMEM((72, L), F32),
-            pltpu.VMEM((72, L), F32),
             pltpu.VMEM((NP, L, 2 * L), BF16),
             pltpu.VMEM((E, R, L), BF16),
             pltpu.VMEM((R * E + E, L), F32),
@@ -380,6 +439,7 @@
             pltpu.VMEM((E * K, R, L), F32),
             pltpu.VMEM((CB, R, L), F32),
             dma((K,)), dma, dma((4,)), dma((2,)), dma((2,)), dma, dma, dma, dma,
+            pltpu.SemaphoreType.REGULAR((2,)), pltpu.SemaphoreType.REGULAR,
         ],
         compiler_params=pltpu.CompilerParams(
             collective_id=0, has_side_effects=True, vmem_limit_bytes=62 * 1024 * 1024),
@@ -393,8 +453,9 @@
             pltpu.VMEM((NG, CAP * R, L), BF16),
             pltpu.SMEM((NG, 1, L), I32),
             pltpu.VMEM((CB + 1, R, L), F32),
+            pltpu.VMEM((CB + 1, R, L), F32),
             pltpu.VMEM((R * CB + CB, L), F32),
-            dma((8,)), dma, dma,
+            dma((4,)), dma, dma,
         ],
         compiler_params=pltpu.CompilerParams(vmem_limit_bytes=62 * 1024 * 1024),
     )(recv, labels, home)

time: 54.1 us -> 46 us (0.85)
  the two profiles are of different devices: /device:TPU:1 before, /device:TPU:209 now
where the time goes in v2:
time: 46 us; the launch traced here: 45.8 us
  Pallas kernels  45.8 us (100%)
    pallas_call x1, Pallas kernels, on_device(): pl.pallas_call(exchange, out_shape=(jax.ShapeDtypeStruct((NG, CAP * R, L)...  42.7 us
    pallas_call x1, Pallas kernels, on_device(): pl.pallas_call(collect, out_shape=jax.ShapeDtypeStruct((CB, 64 * 64), F32...  3.14 us

profile of v2, /device:TPU:209, one launch (start us, length us, event | category | flops | bytes accessed | tf_op | source)
XLA Modules:
  0.0 45.8 jit_solution(16809279394623021325)
XLA Ops:
  0.0 42.7 %shard_map.46 = (bf16[64,64,128]{2,1,0:T(8,128)(2,1)}, s32[64,1,128]{2,1,0:T(1,128)}, f32[32,32,128]{2,1,0:T(8,128)}) custom-call(bf16[7,24,4096]{2,1,0:T(8,128)(2,1)} %bitcast.3, bf16[24,4096]{1,0:T(8,128)(2,1)} %p_ref.1, s32[7,24]{1,0:T(8,128)} %bitcast.4, s32[7,24]{1,0:T(8,128)} %bitcast.5), custom_call_target="tpu_custom_call" | custom-call | tf_op jit(solution)/shard_map/pallas_call | solution.py:415
  42.7 3.1 %shard_map.47 = f32[32,4096]{1,0:T(8,128)} custom-call(bf16[64,64,128]{2,1,0:T(8,128)(2,1)} %get-tuple-element.8.recv_ref, s32[64,1,128]{2,1,0:T(1,128)} %get-tuple-element.9.lab_ref, f32[32,32,128]{2,1,0:T(8,128)} %get-tuple-element.10.home_ref), custom_call_target="tpu_custom_call" | custom-call | tf_op jit(solution)/shard_map/pallas_call | solution.py:447

commit v3 on v2

--- a/solution.py
+++ b/solution.py
@@ -34,7 +34,8 @@
 
 
 def kind_of(dom, g):
-    return jnp.where((dom == 0) & (g == 0), 2, jnp.where(((g >> 1) & 7) == 4, 1, 0))
+    y = (g >> 1) & 7
+    return jnp.where((dom == 0) & (g == 0), 7, jnp.where(y < 4, y, 10 - y))
 
 
 def routing(tgt_v, device):
@@ -113,7 +114,7 @@
     def _():
         pl.semaphore_signal(barrier, inc=1, device_id=(dom - 1, me), device_id_type=MESH)
 
-    @pl.when(has_high & (kind < 2))
+    @pl.when(has_high & (kind < 7))
     def _():
         pl.semaphore_signal(barrier, inc=1, device_id=(dom + 1, me), device_id_type=MESH)
 
@@ -162,45 +163,35 @@
             src_ref=src, dst_ref=dst, send_sem=halo_send.at[i], recv_sem=halo_recv.at[i],
             device_id=(dom + 1 if up else dom - 1, me), device_id_type=MESH)
 
-    def met():
-        early = 7 * 8 - (dom == 0).astype(I32)
-        peers = jnp.where(kind == 0, early - 1, jnp.where(kind == 1, early + 8 - 1, NG - 1))
-        low = (has_low & jnp.logical_not(above_first)).astype(I32)
-        pl.semaphore_wait(barrier, peers + low + has_high.astype(I32))
-
-    def send_halo():
-        @pl.when(has_high)
+    rows = jnp.where(kind < 3, kind + 1, kind + 2)
+    peers = jnp.where(kind == 7, NG - 1, rows * 8 - 1 - (dom == 0).astype(I32))
+    low = (has_low & jnp.logical_not(above_first)).astype(I32)
+    pl.semaphore_wait(barrier, peers + low + has_high.astype(I32))
+
+    @pl.when(has_high)
+    def _():
+        halo(True).start()
+
+    @pl.when(kind == 7)
+    def _():
+        pl.semaphore_signal(late_z, inc=1, device_id=(dom + 1, me), device_id_type=MESH)
+
+    @pl.when(has_low & jnp.logical_not(above_first))
+    def _():
+        halo(False).start()
+
+    here = jnp.where(kind == 7, 8, y)
+
+    def answer(d, c):
+        q = (me + d) & (NG - 1)
+
+        @pl.when(kind_of(dom, q) < kind)
         def _():
-            halo(True).start()
-
-        @pl.when(above_first)
-        def _():
-            pl.semaphore_wait(late_z, 1)
-
-        @pl.when(has_low)
-        def _():
-            halo(False).start()
-
-    @pl.when(kind > 0)
-    def _():
-        met()
-
-        @pl.when(kind == 2)
-        def _():
-            pl.semaphore_signal(late_z, inc=1, device_id=(dom + 1, me), device_id_type=MESH)
-
-        send_halo()
-
-        def answer(d, c):
-            q = (me + d) & (NG - 1)
-
-            @pl.when(kind_of(dom, q) < kind)
-            def _():
-                pl.semaphore_signal(late.at[kind - 1], inc=1, device_id=(dom, q), device_id_type=MESH)
-
-            return c
-
-        lax.fori_loop(1, NG, answer, 0)
+            pl.semaphore_signal(late.at[here], inc=1, device_id=(dom, q), device_id_type=MESH)
+
+        return c
+
+    lax.fori_loop(1, NG, answer, 0)
 
     tgt_copy.wait()
     tab_v[...] = routing(tgt_v, device)
@@ -246,10 +237,10 @@
     col_copy.wait()
     tab_copy.wait()
 
-    @pl.when(kind == 0)
-    def _():
-        met()
-        send_halo()
+    @pl.when(above_first)
+    def _():
+        pl.semaphore_wait(late_z, 1)
+        halo(False).start()
 
     @pl.when(has_low)
     def _():
@@ -298,22 +289,25 @@
             send_v[q, s * R:(s + 1) * R, :] = term(tab_s[s, q]).astype(BF16)
         lab_v[q] = jnp.where(lane == 0, tab_s[2, q], tab_s[3, q])
 
-    ring = (y + 3) & 7
-
     def send(n, c):
-        half, i = n >> 3, n & 7
-        away = jnp.where((i & 1) == 1, (i + 1) >> 1, 7 - (i >> 1))
-        to_y = jnp.where(i == 7, 4, (5 + lax.rem(ring + away, 7)) & 7)
-        peers = []
-        for j in range(4):
-            to_x, to_core = (x + half * 2 + j // 2) & 3, (core + j) & 1
-            peers.append((to_x * 8 + to_y) * 2 + to_core)
+        turn, pair = n >> 2, n & 3
+        dx = (2 - turn) & 3
+        dx = jnp.where(turn == 2, 3, jnp.where(turn == 3, 0, dx))
+        pair = jnp.where(turn == 0, (pair + 1) & 3, pair)
+        to_ys = []
+        for j, far in enumerate(((y + 4 + pair) & 7, (y + 3 - pair) & 7)):
+            i = pair * 2 + j
+            away = jnp.where(i == 0, 2, jnp.where(i == 1, 3, jnp.where(i == 2, 1, jnp.where(i == 3, 4, 0))))
+            by_kind = jnp.where(i > 4, 11 - i, (7 + lax.rem(((y + 1) & 7) + away, 5)) & 7)
+            to_ys.append(jnp.where(turn >= 2, by_kind, far))
+        peers = [(((x + dx) & 3) * 8 + to_y) * 2 + ((core + j) & 1) for to_y in to_ys for j in range(2)]
         for q in peers:
             fill(q)
 
-        @pl.when((n == 7) & (kind == 0))
-        def _():
-            pl.semaphore_wait(late.at[0], 8)
+        for to_y in to_ys:
+            @pl.when((n < 4) & (jnp.where(to_y < 4, to_y, 10 - to_y) > kind))
+            def _():
+                pl.semaphore_wait(late.at[to_y], 8)
 
         for q in peers:
             @pl.when((q != me) & ((dom > 0) | (q > 0)))
@@ -326,7 +320,7 @@
 
     @pl.when((dom == 0) & (me > 0))
     def _():
-        pl.semaphore_wait(late.at[1], 1)
+        pl.semaphore_wait(late.at[8], 1)
         pay(0).start()
         lab(0).start()
 
@@ -439,7 +433,7 @@
             pltpu.VMEM((E * K, R, L), F32),
             pltpu.VMEM((CB, R, L), F32),
             dma((K,)), dma, dma((4,)), dma((2,)), dma((2,)), dma, dma, dma, dma,
-            pltpu.SemaphoreType.REGULAR((2,)), pltpu.SemaphoreType.REGULAR,
+            pltpu.SemaphoreType.REGULAR((9,)), pltpu.SemaphoreType.REGULAR,
         ],
         compiler_params=pltpu.CompilerParams(
             collective_id=0, has_side_effects=True, vmem_limit_bytes=62 * 1024 * 1024),

time: 46 us -> 44.3 us (0.963)
  the two profiles are of different devices: /device:TPU:209 before, /device:TPU:193 now
where the time goes in v3:
time: 44.3 us; the launch traced here: 44.1 us
  Pallas kernels  44.1 us (100%)
    pallas_call x1, Pallas kernels, on_device(): pl.pallas_call(exchange, out_shape=(jax.ShapeDtypeStruct((NG, CAP * R, L)...  41 us
    pallas_call x1, Pallas kernels, on_device(): pl.pallas_call(collect, out_shape=jax.ShapeDtypeStruct((CB, 64 * 64), F32...  3.14 us

profile of v3, /device:TPU:193, one launch (start us, length us, event | category | flops | bytes accessed | tf_op | source)
XLA Modules:
  0.0 44.1 jit_solution(2706031858673852761)
XLA Ops:
  0.0 41.0 %shard_map.46 = (bf16[64,64,128]{2,1,0:T(8,128)(2,1)}, s32[64,1,128]{2,1,0:T(1,128)}, f32[32,32,128]{2,1,0:T(8,128)}) custom-call(bf16[7,24,4096]{2,1,0:T(8,128)(2,1)} %bitcast.3, bf16[24,4096]{1,0:T(8,128)(2,1)} %p_ref.1, s32[7,24]{1,0:T(8,128)} %bitcast.4, s32[7,24]{1,0:T(8,128)} %bitcast.5), custom_call_target="tpu_custom_call" | custom-call | tf_op jit(solution)/shard_map/pallas_call | solution.py:409
  41.0 3.1 %shard_map.47 = f32[32,4096]{1,0:T(8,128)} custom-call(bf16[64,64,128]{2,1,0:T(8,128)(2,1)} %get-tuple-element.8.recv_ref, s32[64,1,128]{2,1,0:T(1,128)} %get-tuple-element.9.lab_ref, f32[32,32,128]{2,1,0:T(8,128)} %get-tuple-element.10.home_ref), custom_call_target="tpu_custom_call" | custom-call | tf_op jit(solution)/shard_map/pallas_call | solution.py:441

commit v4 on v3

--- a/solution.py
+++ b/solution.py
@@ -105,8 +105,13 @@
     has_high = dom < doms - 1
     above_first = (dom == 1) & (me == 0)
 
-    p_copy = pltpu.make_async_copy(p_ref, p_v, p_sem)
-    p_copy.start()
+    half = 64 * 64 // 2
+    p_copies = [
+        pltpu.make_async_copy(p_ref.at[:, pl.ds(i * half, half)], p_v.at[:, pl.ds(i * half, half)], p_sem.at[i])
+        for i in range(2)
+    ]
+    for c in p_copies:
+        c.start()
 
     barrier = pltpu.get_barrier_semaphore()
 
@@ -137,15 +142,12 @@
     for c in a_copies:
         c.start()
 
-    p_copy.wait()
     for r in range(R):
+        if r % (R // 2) == 0:
+            p_copies[r // (R // 2)].wait()
         pf[pl.ds(r * E, E), :] = p_v[:, r * L:(r + 1) * L].astype(F32)
-
-    def own(e, c):
+    for e in [*range(HALO), *range(E - HALO, E)]:
         p2[HALO + e] = pf[pl.ds(e, R, stride=E), :].astype(BF16)
-        return c
-
-    lax.fori_loop(0, E, own, 0, unroll=8)
 
     @pl.when(jnp.logical_not(has_low))
     def _():
@@ -255,7 +257,7 @@
         spread_block(at, p2[at].astype(F32))
         return c
 
-    lax.fori_loop(0, 2 * HALO, prepare_halo, 0, unroll=4)
+    lax.fori_loop(0, 2 * HALO, prepare_halo, 0, unroll=12)
 
     first_own = device * E
 
@@ -371,7 +373,7 @@
     all_pay().wait()
 
 
-def collect(recv_ref, lab_ref, home_ref, out_ref, recv_v, lab_s, acc, acc_b, turned, rsem, lsem, hsem):
+def collect(recv_ref, lab_ref, home_ref, out_ref, recv_v, lab_s, acc, acc_b, turned, out_v, rsem, lsem, hsem, osem):
     me = lax.axis_index("grp")
     lab_copy = pltpu.make_async_copy(lab_ref, lab_s, lsem)
     lab_copy.start()
@@ -392,15 +394,18 @@
 
     for i in range(4):
         copies[i].wait()
-        lax.fori_loop(i * 16, i * 16 + 16, add, 0, unroll=8)
-
-    def turn(t, c):
-        turned[pl.ds(t, R, stride=CB), :] = acc[t] + acc_b[t]
-        return c
-
-    lax.fori_loop(0, CB, turn, 0, unroll=8)
-    for r in range(R):
-        out_ref[:, r * L:(r + 1) * L] = turned[r * CB:(r + 1) * CB, :]
+        lax.fori_loop(i * 16, i * 16 + 16, add, 0, unroll=16)
+
+    outs = []
+    for g in range(0, CB, 8):
+        for t in range(g, g + 8):
+            turned[pl.ds(t, R, stride=CB), :] = acc[t] + acc_b[t]
+        for r in range(R):
+            out_v[g:g + 8, r * L:(r + 1) * L] = turned[r * CB + g:r * CB + g + 8, :]
+        outs.append(pltpu.make_async_copy(out_v.at[pl.ds(g, 8)], out_ref.at[pl.ds(g, 8)], osem.at[g // 8]))
+        outs[-1].start()
+    for c in outs:
+        c.wait()
 
 
 def on_device(a_blocks, p_blocks, columns, targets):
@@ -432,7 +437,7 @@
             pltpu.VMEM((NG, 1, L), I32),
             pltpu.VMEM((E * K, R, L), F32),
             pltpu.VMEM((CB, R, L), F32),
-            dma((K,)), dma, dma((4,)), dma((2,)), dma((2,)), dma, dma, dma, dma,
+            dma((K,)), dma((2,)), dma((4,)), dma((2,)), dma((2,)), dma, dma, dma, dma,
             pltpu.SemaphoreType.REGULAR((9,)), pltpu.SemaphoreType.REGULAR,
         ],
         compiler_params=pltpu.CompilerParams(
@@ -442,14 +447,15 @@
         collect,
         out_shape=jax.ShapeDtypeStruct((CB, 64 * 64), F32),
         in_specs=[hbm] * 3,
-        out_specs=pl.BlockSpec(memory_space=pltpu.VMEM),
+        out_specs=hbm,
         scratch_shapes=[
             pltpu.VMEM((NG, CAP * R, L), BF16),
             pltpu.SMEM((NG, 1, L), I32),
             pltpu.VMEM((CB + 1, R, L), F32),
             pltpu.VMEM((CB + 1, R, L), F32),
             pltpu.VMEM((R * CB + CB, L), F32),
-            dma((4,)), dma, dma,
+            pltpu.VMEM((CB, 64 * 64), F32),
+            dma((4,)), dma, dma, dma((4,)),
         ],
         compiler_params=pltpu.CompilerParams(vmem_limit_bytes=62 * 1024 * 1024),
     )(recv, labels, home)

time: 44.3 us -> 43.7 us (0.986)
  Pallas kernels: 44.1 us -> 43.6 us
where the time goes in v4:
time: 43.7 us; the launch traced here: 43.6 us
  Pallas kernels  43.6 us (100%)
    pallas_call x1, Pallas kernels, on_device(): pl.pallas_call(exchange, out_shape=(jax.ShapeDtypeStruct((NG, CAP * R, L)...  40.6 us
    pallas_call x1, Pallas kernels, on_device(): pl.pallas_call(collect, out_shape=jax.ShapeDtypeStruct((CB, 64 * 64), F32...  2.99 us

profile of v4, /device:TPU:193, one launch (start us, length us, event | category | flops | bytes accessed | tf_op | source)
XLA Modules:
  0.0 43.6 jit_solution(12222174765176502338)
XLA Ops:
  0.0 40.6 %shard_map.46 = (bf16[64,64,128]{2,1,0:T(8,128)(2,1)}, s32[64,1,128]{2,1,0:T(1,128)}, f32[32,32,128]{2,1,0:T(8,128)}) custom-call(bf16[7,24,4096]{2,1,0:T(8,128)(2,1)} %bitcast.3, bf16[24,4096]{1,0:T(8,128)(2,1)} %p_ref.1, s32[7,24]{1,0:T(8,128)} %bitcast.4, s32[7,24]{1,0:T(8,128)} %bitcast.5), custom_call_target="tpu_custom_call" | custom-call | tf_op jit(solution)/shard_map/pallas_call | solution.py:414
  40.6 3.0 %shard_map.47 = f32[32,4096]{1,0:T(8,128)} custom-call(bf16[64,64,128]{2,1,0:T(8,128)(2,1)} %get-tuple-element.8.recv_ref, s32[64,1,128]{2,1,0:T(1,128)} %get-tuple-element.9.lab_ref, f32[32,32,128]{2,1,0:T(8,128)} %get-tuple-element.10.home_ref), custom_call_target="tpu_custom_call" | custom-call | tf_op jit(solution)/shard_map/pallas_call | solution.py:446

commit v5 on v4

--- a/solution.py
+++ b/solution.py
@@ -299,8 +299,7 @@
         to_ys = []
         for j, far in enumerate(((y + 4 + pair) & 7, (y + 3 - pair) & 7)):
             i = pair * 2 + j
-            away = jnp.where(i == 0, 2, jnp.where(i == 1, 3, jnp.where(i == 2, 1, jnp.where(i == 3, 4, 0))))
-            by_kind = jnp.where(i > 4, 11 - i, (7 + lax.rem(((y + 1) & 7) + away, 5)) & 7)
+            by_kind = jnp.where(i < 3, i, jnp.where(i == 3, 7, jnp.where(i == 4, 3, 11 - i)))
             to_ys.append(jnp.where(turn >= 2, by_kind, far))
         peers = [(((x + dx) & 3) * 8 + to_y) * 2 + ((core + j) & 1) for to_y in to_ys for j in range(2)]
         for q in peers:
@@ -314,8 +313,8 @@
         for q in peers:
             @pl.when((q != me) & ((dom > 0) | (q > 0)))
             def _():
+                lab(q).start()
                 pay(q).start()
-                lab(q).start()
         return c
 
     lax.fori_loop(0, 16, send, 0)
@@ -323,8 +322,8 @@
     @pl.when((dom == 0) & (me > 0))
     def _():
         pl.semaphore_wait(late.at[8], 1)
+        lab(0).start()
         pay(0).start()
-        lab(0).start()
 
     def at_home(i, acc):
         n = i * 8

time: 43.7 us -> 43.6 us (level)
  the two profiles are of different devices: /device:TPU:193 before, /device:TPU:209 now
where the time goes in v5:
time: 43.6 us; the launch traced here: 43.4 us
  Pallas kernels  43.4 us (100%)
    pallas_call x1, Pallas kernels, on_device(): pl.pallas_call(exchange, out_shape=(jax.ShapeDtypeStruct((NG, CAP * R, L)...  40.4 us
    pallas_call x1, Pallas kernels, on_device(): pl.pallas_call(collect, out_shape=jax.ShapeDtypeStruct((CB, 64 * 64), F32...  3 us

profile of v5, /device:TPU:209, one launch (start us, length us, event | category | flops | bytes accessed | tf_op | source)
XLA Modules:
  0.0 43.4 jit_solution(18195720664293603995)
XLA Ops:
  0.0 40.4 %shard_map.46 = (bf16[64,64,128]{2,1,0:T(8,128)(2,1)}, s32[64,1,128]{2,1,0:T(1,128)}, f32[32,32,128]{2,1,0:T(8,128)}) custom-call(bf16[7,24,4096]{2,1,0:T(8,128)(2,1)} %bitcast.3, bf16[24,4096]{1,0:T(8,128)(2,1)} %p_ref.1, s32[7,24]{1,0:T(8,128)} %bitcast.4, s32[7,24]{1,0:T(8,128)} %bitcast.5), custom_call_target="tpu_custom_call" | custom-call | tf_op jit(solution)/shard_map/pallas_call | solution.py:413
  40.5 3.0 %shard_map.47 = f32[32,4096]{1,0:T(8,128)} custom-call(bf16[64,64,128]{2,1,0:T(8,128)(2,1)} %get-tuple-element.8.recv_ref, s32[64,1,128]{2,1,0:T(1,128)} %get-tuple-element.9.lab_ref, f32[32,32,128]{2,1,0:T(8,128)} %get-tuple-element.10.home_ref), custom_call_target="tpu_custom_call" | custom-call | tf_op jit(solution)/shard_map/pallas_call | solution.py:445
